TPU v7x, 256 devices: a whole 4x4x8 slice. The times are simulated.
256 devices in a mesh: dp: 32 (over z, x), tensor: 8 (over y, core).
Axes of the slice: x: 4, y: 4, z: 8, core: 2. Of those that a mesh axis runs over, the one named last changes fastest.
Arguments:
- up_grad: bfloat16 [8192, 14336], P('dp', 'tensor'), may hold values from -6 to 6
- up_error: float32 [8192, 14336], P('dp', 'tensor'), may hold values from -6 to 6
- up_basis: float32 [14336, 64], P('tensor'), may hold values from -0.046875 to 0.046875
- down_grad: bfloat16 [14336, 8192], P('tensor', 'dp'), may hold values from -6 to 6
- down_error: float32 [14336, 8192], P('tensor', 'dp'), may hold values from -6 to 6
- down_basis: float32 [8192, 64], P('dp'), may hold values from -0.0625 to 0.0625
Outputs:
- up_residual: float32 [8192, 14336], P('dp', 'tensor')
- down_residual: float32 [14336, 8192], P('tensor', 'dp')
- up_left: float32 [8192, 64], P('dp')
- up_right: float32 [14336, 64], P('tensor')
- down_left: float32 [14336, 64], P('tensor')
- down_right: float32 [8192, 64], P('dp')
All inputs are finite; a program needn't handle non-finite values.
Results may differ from a plain program's by a relative error of at most 0.0003.
Values sent between devices are 32-bit elements; how exact they have to be, the bound alone decides.
A program may use at most 64 MiB of HBM per device.

v0:
```python
import jax
import jax.numpy as jnp
from jax import lax
from jax.sharding import PartitionSpec as P

highest = lax.Precision.HIGHEST


def product(left, right):
    return jnp.dot(left, right, precision=highest, preferred_element_type=jnp.float32)


def factor_basis(matrix, gram):
    lower = jnp.linalg.cholesky(gram)
    return lax.linalg.triangular_solve(lower, matrix, left_side=False, lower=True, transpose_a=True)


def on_device(up_grad, up_error, up_basis, down_grad, down_error, down_basis):
    up_acc = up_grad.astype(jnp.float32) + up_error
    down_acc = down_grad.astype(jnp.float32) + down_error
    up_part = product(up_acc, up_basis)
    down_part = product(down_acc, down_basis)
    up_sum = lax.psum(up_part, "tensor")
    up_gram = lax.psum(product(up_sum.T, up_sum), "dp")
    up_hat = factor_basis(up_sum, up_gram)
    up_fac = lax.psum(product(up_acc.T, up_hat), "dp")
    down_sum = lax.psum(down_part, "dp")
    down_gram = lax.psum(product(down_sum.T, down_sum), "tensor")
    down_hat = factor_basis(down_sum, down_gram)
    down_fac = lax.psum(product(down_acc.T, down_hat), "tensor")
    up_res = up_acc - product(up_hat, up_fac.T)
    down_res = down_acc - product(down_hat, down_fac.T)
    return (up_res, down_res, up_hat, up_fac, down_hat, down_fac)


def solution(mesh):
    placed = (
        P("dp", "tensor"),
        P("dp", "tensor"),
        P("tensor", None),
        P("tensor", "dp"),
        P("tensor", "dp"),
        P("dp", None),
    )
    return jax.shard_map(
        on_device,
        mesh=mesh,
        in_specs=placed,
        out_specs=(
            P("dp", "tensor"),
            P("tensor", "dp"),
            P("dp", None),
            P("tensor", None),
            P("tensor", None),
            P("dp", None),
        ),
        check_vma=False,
    )
```

profile of v0, /device:TPU:1, one launch (start us, length us, event | category | flops | bytes accessed | tf_op | source)
XLA Modules:
  0.0 495.8 jit_solution(11569755991922127702)
XLA Ops:
  7.2 1.0 copy-done
  8.2 4.2 fusion.1
  12.5 4.6 fusion.3
  17.1 61.1 %all-reduce.5.cloned.1.call-done = f32[256,64]{0,1:T(8,128)} async-done(((f32[256,64]{0,1:T(8,128)}), f32[256,64]{0,1:T(8,128)}) %all-reduce.5.cloned.1.call-update) | async-done | bytes 65552 | tf_op jit(solution)/shard_map/psum | solution.py:23
  78.1 1.1 fusion.12
  79.3 115.6 %psum.43 = f32[64,64]{0,1:T(8,128)S(1)} all-reduce(f32[64,64]{0,1:T(8,128)S(1)} %fusion.12), channel_id=1, replica_groups=mesh['dp'=32,'tensor'=8] {'dp'}, use_global_device_ids=true, to_apply=%region_1.0 | all-reduce | flops 4096 | bytes 32768 | tf_op jit(solution)/shard_map/psum | solution.py:24
  194.9 5.8 %cholesky.44 = f32[64,64]{1,0:T(8,128)S(1)} custom-call(f32[64,64]{1,0:T(8,128)S(1)} %fusion.11), custom_call_target="Cholesky" | custom-call | tf_op jit(solution)/shard_map/jit(cholesky)/cholesky | solution.py:14
  201.5 0.7 fusion.4
  202.1 4.9 custom-call.8
  207.0 1.1 fusion.9
  208.2 2.2 fusion
  210.4 168.0 %all-reduce.9.cloned.1.call-done = (f32[1792,64]{0,1:T(8,128)}, f32[1792,64]{0,1:T(8,128)}) async-done(((f32[1792,64]{0,1:T(8,128)}, f32[1792,64]{0,1:T(8,128)}), (f32[1792,64]{0,1:T(8,128)}, f32[1792,64]{0,1:T(8,128)})) %all-reduce.9.cloned.1.call-update) | async-done | bytes 917520 | tf_op jit(solution)/shard_map/psum | solution.py:26
  378.4 1.7 fusion.13
  380.1 25.8 %psum.46 = f32[64,64]{0,1:T(8,128)S(1)} all-reduce(f32[64,64]{0,1:T(8,128)S(1)} %fusion.13), channel_id=1, replica_groups=mesh['dp'=32,'tensor'=8] {'tensor'}, use_global_device_ids=true, to_apply=%region_6.8 | all-reduce | flops 4096 | bytes 32768 | tf_op jit(solution)/shard_map/psum | solution.py:28
  406.0 5.8 %cholesky.55 = f32[64,64]{1,0:T(8,128)S(1)} custom-call(f32[64,64]{1,0:T(8,128)S(1)} %fusion.8), custom_call_target="Cholesky" | custom-call | tf_op jit(solution)/shard_map/jit(cholesky)/cholesky | solution.py:14
  412.5 0.7 fusion.5
  413.2 4.9 custom-call.9
  418.1 1.6 fusion.6
  419.7 0.8 copy-done.3
  420.4 3.6 fusion.2
  424.1 3.9 convolution_subtract_fusion.1
  428.0 55.0 %all-reduce.7.cloned.1.call-done = f32[256,64]{0,1:T(8,128)} async-done(((f32[256,64]{0,1:T(8,128)}), f32[256,64]{0,1:T(8,128)}) %all-reduce.7.cloned.1.call-update) | async-done | bytes 65552 | tf_op jit(solution)/shard_map/psum | solution.py:30
  483.0 4.8 convolution_subtract_fusion
  487.9 0.8 copy.22
  (29 shorter events, 2.4 us)
Async XLA Ops:
  7.2 1.0 copy-start
  7.2 5.3 %copy-start.7 = (f32[256,64]{0,1:T(8,128)S(1)}, f32[256,64]{0,1:T(8,128)}, u32[]{:S(2)}) copy-start(f32[256,64]{0,1:T(8,128)} %param.12) | copy-start | bytes 196612
  7.2 70.9 %all-reduce.5.cloned.1.call-start = ((), (), s32[]{:S(2)}) async-start(), calls=%async_computation | async-start | bytes 131072 | tf_op jit(solution)/shard_map/psum | solution.py:23
  12.4 195.7 %copy-start.1 = (f32[256,1792]{1,0:T(8,128)S(1)}, f32[256,1792]{1,0:T(8,128)}, u32[]{:S(2)}) copy-start(f32[256,1792]{1,0:T(8,128)} %param.8) | copy-start | bytes 5505028
  12.4 195.7 %copy-start.2 = (bf16[256,1792]{1,0:T(8,128)(2,1)S(1)}, bf16[256,1792]{1,0:T(8,128)(2,1)}, u32[]{:S(2)}) copy-start(bf16[256,1792]{1,0:T(8,128)(2,1)} %param.7) | copy-start | bytes 2752516
  12.4 366.0 %all-reduce.9.cloned.1.call-start = ((), (), s32[]{:S(2)}) async-start(), calls=%async_computation.2 | async-start | bytes 1835008 | tf_op jit(solution)/shard_map/psum | solution.py:26
  208.1 216.0 %copy-start.5 = (f32[256,64]{0,1:T(8,128)}, f32[256,64]{0,1:T(8,128)S(1)}, u32[]{:S(2)}) copy-start(f32[256,64]{0,1:T(8,128)S(1)} %fusion.9) | copy-start | bytes 196612
  210.3 272.7 %all-reduce.7.cloned.1.call-start = ((), (), s32[]{:S(2)}) async-start(), calls=%async_computation.1 | async-start | bytes 131072 | tf_op jit(solution)/shard_map/psum | solution.py:30
  419.7 0.8 copy-start.3
  428.0 59.9 %copy-start.4 = (f32[1792,64]{0,1:T(8,128)S(1)}, f32[1792,64]{0,1:T(8,128)}, u32[]{:S(2)}) copy-start(f32[1792,64]{0,1:T(8,128)} %get-tuple-element.12) | copy-start | bytes 1376260
  483.0 5.6 %copy-start.6 = (f32[256,64]{0,1:T(8,128)S(1)}, f32[256,64]{0,1:T(8,128)}, u32[]{:S(2)}) copy-start(f32[256,64]{0,1:T(8,128)} %all-reduce.7.cloned.1.call-done) | copy-start | bytes 196612
Sparse Core Ops, SparseCore 0:
  12.5 65.5 all-reduce.4
  210.5 167.9 all-reduce.8
  424.2 58.7 all-reduce.6
where the time goes:
time: 498 us; the launch traced here: 496 us
  waiting for transfers between devices  284 us (57%)
  blocking collectives  141 us (28%)
  matrix products  28.8 us (6%)
  other arithmetic  24.2 us (5%)
  between operations  13.9 us (3%)
    psum x1, waiting for transfers between devices, on_device(): up_fac = lax.psum(product(up_acc.T, up_hat), 'dp')  168 us
    psum x1, blocking collectives, on_device(): up_gram = lax.psum(product(up_sum.T, up_sum), 'dp')  116 us
    psum x1, waiting for transfers between devices, on_device(): up_sum = lax.psum(up_part, 'tensor')  61.1 us
    psum x1, waiting for transfers between devices, on_device(): down_fac = lax.psum(product(down_acc.T, down_hat), 'tensor')  55 us
    dot_general x8, matrix products, product(): jnp.dot(left, right, precision=highest, preferred_element_type=jnp.float32)  26.1 us
    psum x1, blocking collectives, on_device(): down_gram = lax.psum(product(down_sum.T, down_sum), 'tensor')  25.8 us
    another operation x6, other arithmetic, factor_basis(): lower = jnp.linalg.cholesky(gram)  13 us
    another operation x4, other arithmetic, factor_basis(): lax.linalg.triangular_solve(lower, matrix, left_side=False, lower=True, t...  11.1 us
  transfers between devices with their start and end apart: 3, of which 3 were waited for; matrix products, arithmetic and copies ran while one was open for 2% of the time, Pallas kernels for 0%

commit v1 on v0

v1 whole, which is shorter than its diff:
```python
import jax
import jax.numpy as jnp
from jax import lax
from jax.experimental import pallas as pl
from jax.experimental.pallas import tpu as pltpu
from jax.sharding import PartitionSpec as P

MESH = pl.DeviceIdType.MESH
F32 = jnp.float32
BF16 = jnp.bfloat16
BLK = 256
NB = 7
RANK = 64
NZ, NX, NY, NC = 8, 4, 4, 2
SUB = RANK // NX


def split(a):
    hi = a.astype(BF16)
    lo = (a - hi.astype(F32)).astype(BF16)
    return hi, lo


def dot(a, b, dims):
    return lax.dot_general(a, b, (dims, ((), ())), preferred_element_type=F32)


NN = ((1,), (0,))
NT = ((1,), (1,))
TN = ((0,), (0,))


def product3(cat, hi_part, right_hi, right_lo, dims):
    both = dot(cat, right_hi, dims)
    return both[:RANK] + both[RANK:] + dot(hi_part, right_lo, dims)


def gram(cat):
    c = dot(cat, cat, NT)
    return c[:RANK, :RANK] + c[:RANK, RANK:] + c[RANK:, :RANK] + c[RANK:, RANK:]


def pack(g):
    return jnp.concatenate([g[:32], g[32:]], axis=1)


def unpack(p):
    return jnp.concatenate([p[:, :RANK], p[:, RANK:]], axis=0)


def inverse_factor(g):
    sub = lax.broadcasted_iota(jnp.int32, (8, 128), 0)
    lane = lax.broadcasted_iota(jnp.int32, (8, 128), 1)
    groups = []
    for i in range(8):
        eye = (lane[:, :RANK] == sub[:, :RANK] + 8 * i).astype(F32)
        groups.append(jnp.concatenate([eye, g[8 * i : 8 * i + 8]], axis=1))
    scales = [jnp.ones((8, 128), F32) for _ in range(8)]
    for k in range(RANK):
        b, r = k // 8, k % 8
        row = jnp.broadcast_to(groups[b][r : r + 1, :], (8, 128))
        pivot = jnp.broadcast_to(groups[b][r : r + 1, RANK + k : RANK + k + 1], (8, 128))
        scales[b] = jnp.where(sub == r, 1.0 / jnp.sqrt(pivot), scales[b])
        scaled = row * (1.0 / pivot)
        for i in range(b, 8):
            col = jnp.broadcast_to(groups[i][:, RANK + k : RANK + k + 1], (8, 128))
            if i == b:
                col = jnp.where(sub > r, col, 0.0)
            groups[i] = groups[i] - col * scaled
    return jnp.concatenate([groups[i][:, :RANK] * scales[i][:, :RANK] for i in range(8)], axis=0)


def triple_left(a):
    hi, lo = split(a)
    return jnp.concatenate([hi, lo, hi], axis=1)


def triple_right(a):
    hi, lo = split(a)
    return jnp.concatenate([hi, hi, lo], axis=0)


def wait_bytes(ref, sem):
    pltpu.make_async_copy(ref, ref, sem).wait()


def kernel(
    gu, eu, bu, gd, ed, bd,
    ru, rd, lu, wu, ld, wd,
    gub, eub, uh, ul, gdb, edb, dh, dl, bub, bdb,
    src, rx, tx, zrx, out,
    part, crx, half, yb, gpart, gx, gz, gsum, gt,
    sem_load, sem_store, sem_base,
    s_x, s_z, s_ag, r_x, r_z, r_zag, r_xag,
    s_c, r_c, s_y, r_y, s_g, r_g,
):
    dp = lax.axis_index("dp")
    t = lax.axis_index("tensor")
    z, x = dp // NX, dp % NX
    y, c = t // NC, t % NC

    def to_x(d):
        return (z * NX + lax.rem(x + d, NX), t)

    def to_z(target):
        return (target * NX + x, t)

    def to_t(dy, dc):
        return (dp, lax.rem(y + dy, NY) * NC + lax.rem(c + dc, NC))

    others_t = [(dy, dc) for dy in (2, 1, 3, 0) for dc in range(NC) if (dy, dc) != (0, 0)]

    barrier = pltpu.get_barrier_semaphore()
    peers = [to_z(lax.rem(z + d, NZ)) for d in (4, 3, 5, 2, 6, 1, 7)]
    peers += [to_x(d) for d in (2, 1, 3)] + [to_t(*o) for o in others_t]
    for peer in peers:
        pl.semaphore_signal(barrier, inc=1, device_id=peer, device_id_type=MESH)

    skip = (NZ - 1) - z
    at = jnp.where(skip >= 4, 2 * (skip - 4), 2 * (4 - skip) - 1)
    order = []
    for i in range(NB):
        ip = i + jnp.where(i >= at, 1, 0)
        dz = jnp.where(lax.rem(ip, 2) == 1, 4 - (ip + 1) // 2, 4 + ip // 2)
        order.append(lax.rem(z + dz, NZ))
    owner = z < NB
    rows = pl.ds(pl.multiple_of(x * SUB, SUB), SUB)

    def copy_to(a, b, send, recv, device):
        pltpu.make_async_remote_copy(
            src_ref=a, dst_ref=b, send_sem=send, recv_sem=recv, device_id=device, device_id_type=MESH
        ).start()

    base_d = pltpu.make_async_copy(bd, bdb, sem_base.at[0])
    base_d.start()
    loads_d = []
    for i in range(NB):
        cut = pl.ds(pl.multiple_of(order[i] * BLK, BLK), BLK)
        a = pltpu.make_async_copy(gd.at[cut, :], gdb.at[order[i]], sem_load.at[0, i])
        b = pltpu.make_async_copy(ed.at[cut, :], edb.at[order[i]], sem_load.at[1, i])
        a.start()
        b.start()
        loads_d.append((a, b))
    base_u = pltpu.make_async_copy(bu, bub, sem_base.at[1])
    base_u.start()
    loads_u = []
    for j in range(NB):
        cut = pl.ds(j * BLK, BLK)
        a = pltpu.make_async_copy(gu.at[:, cut], gub.at[j], sem_load.at[2, j])
        b = pltpu.make_async_copy(eu.at[:, cut], eub.at[j], sem_load.at[3, j])
        a.start()
        b.start()
        loads_u.append((a, b))

    def x_send(a, i):
        j = order[i]
        for d in (2, 1, 3):
            there = pl.ds(pl.multiple_of(lax.rem(x + d, NX) * SUB, SUB), SUB)
            copy_to(src.at[a, j, there], rx.at[a, i, d - 1], s_x.at[a], r_x.at[a, i], to_x(d))

    def z_send(a, i):
        j = order[i]
        wait_bytes(rx.at[a, i], r_x.at[a, i])
        total = src[a, j, rows, :] + rx[a, i, 0] + rx[a, i, 1] + rx[a, i, 2]
        if i < NB - 1:
            tx[a, i] = total
            copy_to(tx.at[a, i], zrx.at[a, z], s_z.at[a], r_z.at[a], to_z(j))
        else:

            @pl.when(owner)
            def _():
                zrx[a, z] = total

            @pl.when(jnp.logical_not(owner))
            def _():
                tx[a, i] = total
                copy_to(tx.at[a, i], zrx.at[a, z], s_z.at[a], r_z.at[a], to_z(j))

    def reduce_gather(a):
        @pl.when(owner)
        def _():
            wait_bytes(zrx.at[a, pl.ds(0, 7)], r_z.at[a])
            total = zrx[a, 0]
            for s in range(1, NZ):
                total = total + zrx[a, s]
            out[a, z, rows, :] = total
            mine = out.at[a, z, rows]
            for d in (4, 3, 5, 2, 6, 1, 7):
                copy_to(mine, mine, s_ag.at[a], r_zag.at[a, z], to_z(lax.rem(z + d, NZ)))

    def forward(a, i):
        j = order[i]
        block = out.at[a, j, rows]

        def arrive():
            wait_bytes(block, r_zag.at[a, j])

        if i < NB - 1:
            arrive()
        else:
            pl.when(jnp.logical_not(owner))(arrive)
        for d in (2, 1, 3):
            copy_to(block, block, s_ag.at[a], r_xag.at[a, j], to_x(d))

    def gathered(a, i):
        wait_bytes(rx.at[a, 0], r_xag.at[a, order[i]])

    def dp_sends_done(a):
        wait_bytes(rx.at[a], s_x.at[a])
        wait_bytes(rx.at[a], s_ag.at[a])

        @pl.when(owner)
        def _():
            wait_bytes(zrx.at[a, pl.ds(0, 6)], s_z.at[a])
            wait_bytes(zrx.at[a, pl.ds(0, 7)], s_ag.at[a])

        @pl.when(jnp.logical_not(owner))
        def _():
            wait_bytes(zrx.at[a, pl.ds(0, 7)], s_z.at[a])

    def c_send(a):
        copy_to(part.at[a, 1 - c], crx.at[a], s_c.at[a], r_c.at[a], to_t(0, 1))

    def y_send(a):
        wait_bytes(crx.at[a], r_c.at[a])
        total = part[a, c] + crx[a]
        half[a] = total
        yb[a, c * NY + y] = total
        for dy, dc in others_t:
            copy_to(half.at[a], yb.at[a, c * NY + y], s_y.at[a], r_y.at[a], to_t(dy, dc))

    def y_sum(a):
        wait_bytes(yb.at[a, pl.ds(0, 7)], r_y.at[a])
        halves = []
        for h in range(2):
            total = yb[a, h * 4]
            for s in range(1, 4):
                total = total + yb[a, h * 4 + s]
            halves.append(total)
        return jnp.concatenate(halves, axis=0)

    base_d.wait()
    bd_hi, bd_lo = split(bdb[...])
    bd_cat = jnp.concatenate([bd_hi, bd_lo], axis=0)
    for i in range(NB):
        j = order[i]
        loads_d[i][0].wait()
        loads_d[i][1].wait()
        acc = gdb[j].astype(F32) + edb[j]
        edb[j] = acc
        hi, lo = split(acc)
        dh[j] = hi
        dl[j] = lo
        src[0, j] = product3(bd_cat, bd_hi, hi, lo, NT)
    pl.semaphore_wait(barrier, len(peers))
    for i in range(NB):
        x_send(0, i)

    base_u.wait()
    total = jnp.zeros((RANK, BLK), F32)
    for j in range(NB):
        loads_u[j][0].wait()
        loads_u[j][1].wait()
        acc = gub[j].astype(F32) + eub[j]
        eub[j] = acc
        hi, lo = split(acc)
        uh[j] = hi
        ul[j] = lo
        b_hi, b_lo = split(bub[:, j * BLK : (j + 1) * BLK])
        total = total + product3(jnp.concatenate([b_hi, b_lo], axis=0), b_hi, hi, lo, NT)
    part[0, 0] = total[:32]
    part[0, 1] = total[32:]
    c_send(0)
    y_send(0)

    for i in range(NB):
        z_send(0, i)

    xu = y_sum(0)
    xu_hi, xu_lo = split(xu)
    xu_cat = jnp.concatenate([xu_hi, xu_lo], axis=0)
    g = pack(gram(xu_cat))
    gpart[0] = g
    gx[x] = g
    for d in (2, 1, 3):
        copy_to(gpart.at[0], gx.at[x], s_g.at[0], r_g.at[0], to_x(d))
    for i in range(NB):
        j = order[i]
        src[1, j] = product3(xu_cat, xu_hi, uh[j], ul[j], NN)
        x_send(1, i)

    reduce_gather(0)

    wait_bytes(gx.at[pl.ds(0, 3)], r_g.at[0])
    g = gx[0] + gx[1] + gx[2] + gx[3]
    gsum[...] = g
    gz[z] = g
    for d in (4, 3, 5, 2, 6, 1, 7):
        copy_to(gsum, gz.at[z], s_g.at[1], r_g.at[1], to_z(lax.rem(z + d, NZ)))

    for i in reversed(range(NB)):
        forward(0, i)
    for i in range(NB):
        z_send(1, i)

    prod = jnp.zeros((RANK, BLK), F32)
    gsq = jnp.zeros((RANK, RANK), F32)
    for i in reversed(range(NB)):
        gathered(0, i)
    for j in range(NB):
        hi, lo = split(out[0, j])
        cat = jnp.concatenate([hi, lo], axis=0)
        gsq = gsq + gram(cat)
        prod = prod + product3(cat, hi, dh[j], dl[j], NN)
    g = pack(gsq)
    gpart[1] = g
    gt[t] = g
    for dy, dc in others_t:
        copy_to(gpart.at[1], gt.at[t], s_g.at[2], r_g.at[2], to_t(dy, dc))
    part[1, 0] = prod[:32]
    part[1, 1] = prod[32:]
    c_send(1)

    reduce_gather(1)
    y_send(1)

    wait_bytes(gz.at[pl.ds(0, 7)], r_g.at[1])
    g = gz[0]
    for s in range(1, NZ):
        g = g + gz[s]
    inv_u = triple_left(inverse_factor(unpack(g)))
    left_u = dot(inv_u, triple_right(xu), NN)
    lu[...] = left_u
    left_u_t = triple_left(left_u.T)

    for i in reversed(range(NB)):
        forward(1, i)

    wait_bytes(gt.at[pl.ds(0, 7)], r_g.at[2])
    g = gt[0]
    for s in range(1, NY * NC):
        g = g + gt[s]
    inv_d = triple_left(inverse_factor(unpack(g)))
    right_d = dot(inv_d, triple_right(y_sum(1)), NN)
    wd[...] = right_d
    right_d3 = triple_right(right_d)
    stores = []
    for j in range(NB):
        left = dot(inv_d, triple_right(out[0, j]), NN)
        ld[:, j * BLK : (j + 1) * BLK] = left
        edb[j] = edb[j] - dot(triple_left(left.T), right_d3, NN)
        store = pltpu.make_async_copy(edb.at[j], rd.at[pl.ds(j * BLK, BLK), :], sem_store.at[0, j])
        store.start()
        stores.append(store)

    for i in reversed(range(NB)):
        gathered(1, i)
    for j in range(NB):
        right = dot(inv_u, triple_right(out[1, j]), NN)
        wu[:, j * BLK : (j + 1) * BLK] = right
        eub[j] = eub[j] - dot(left_u_t, triple_right(right), NN)
        store = pltpu.make_async_copy(eub.at[j], ru.at[:, pl.ds(j * BLK, BLK)], sem_store.at[1, j])
        store.start()
        stores.append(store)

    dp_sends_done(0)
    dp_sends_done(1)
    for a in range(2):
        wait_bytes(crx.at[a], s_c.at[a])
        wait_bytes(yb.at[a, pl.ds(0, 7)], s_y.at[a])
    wait_bytes(gz.at[pl.ds(0, 3)], s_g.at[0])
    wait_bytes(gz.at[pl.ds(0, 7)], s_g.at[1])
    wait_bytes(gz.at[pl.ds(0, 7)], s_g.at[2])
    for store in stores:
        store.wait()


def on_device(up_grad, up_error, up_basis, down_grad, down_error, down_basis):
    any_space = pl.BlockSpec(memory_space=pl.ANY)
    vmem = pl.BlockSpec(memory_space=pltpu.VMEM)
    dma = pltpu.SemaphoreType.DMA
    wide = NB * BLK
    ru, rd, lu, wu, ld, wd = pl.pallas_call(
        kernel,
        out_shape=(
            jax.ShapeDtypeStruct((BLK, wide), F32),
            jax.ShapeDtypeStruct((wide, BLK), F32),
            jax.ShapeDtypeStruct((RANK, BLK), F32),
            jax.ShapeDtypeStruct((RANK, wide), F32),
            jax.ShapeDtypeStruct((RANK, wide), F32),
            jax.ShapeDtypeStruct((RANK, BLK), F32),
        ),
        in_specs=[any_space] * 6,
        out_specs=(any_space, any_space, vmem, vmem, vmem, vmem),
        scratch_shapes=[
            pltpu.VMEM((NB, BLK, BLK), BF16),
            pltpu.VMEM((NB, BLK, BLK), F32),
            pltpu.VMEM((NB, BLK, BLK), BF16),
            pltpu.VMEM((NB, BLK, BLK), BF16),
            pltpu.VMEM((NB, BLK, BLK), BF16),
            pltpu.VMEM((NB, BLK, BLK), F32),
            pltpu.VMEM((NB, BLK, BLK), BF16),
            pltpu.VMEM((NB, BLK, BLK), BF16),
            pltpu.VMEM((RANK, wide), F32),
            pltpu.VMEM((RANK, BLK), F32),
            pltpu.VMEM((2, NB, RANK, BLK), F32),
            pltpu.VMEM((2, NB, 3, SUB, BLK), F32),
            pltpu.VMEM((2, NB, SUB, BLK), F32),
            pltpu.VMEM((2, NZ, SUB, BLK), F32),
            pltpu.VMEM((2, NB, RANK, BLK), F32),
            pltpu.VMEM((2, 2, RANK // 2, BLK), F32),
            pltpu.VMEM((2, RANK // 2, BLK), F32),
            pltpu.VMEM((2, RANK // 2, BLK), F32),
            pltpu.VMEM((2, 8, RANK // 2, BLK), F32),
            pltpu.VMEM((2, RANK // 2, 128), F32),
            pltpu.VMEM((NX, RANK // 2, 128), F32),
            pltpu.VMEM((NZ, RANK // 2, 128), F32),
            pltpu.VMEM((RANK // 2, 128), F32),
            pltpu.VMEM((NY * NC, RANK // 2, 128), F32),
            dma((4, NB)),
            dma((2, NB)),
            dma((2,)),
            dma((2,)),
            dma((2,)),
            dma((2,)),
            dma((2, NB)),
            dma((2,)),
            dma((2, NB)),
            dma((2, NB)),
            dma((2,)),
            dma((2,)),
            dma((2,)),
            dma((2,)),
            dma((3,)),
            dma((3,)),
        ],
        compiler_params=pltpu.CompilerParams(
            collective_id=0, has_side_effects=True, vmem_limit_bytes=32 * 2**20
        ),
    )(up_grad, up_error, up_basis.T, down_grad, down_error, down_basis.T)
    return ru, rd, lu.T, wu.T, ld.T, wd.T


def solution(mesh):
    placed = (
        P("dp", "tensor"),
        P("dp", "tensor"),
        P("tensor", None),
        P("tensor", "dp"),
        P("tensor", "dp"),
        P("dp", None),
    )
    return jax.shard_map(
        on_device,
        mesh=mesh,
        in_specs=placed,
        out_specs=(
            P("dp", "tensor"),
            P("tensor", "dp"),
            P("dp", None),
            P("tensor", None),
            P("tensor", None),
            P("dp", None),
        ),
        check_vma=False,
    )
```

time: 498 us -> 72.7 us (0.15)
  waiting for transfers between devices: 284 us -> 0 us
  blocking collectives: 141 us -> 0 us
  Pallas kernels: 0 us -> 59.3 us
  matrix products: 28.8 us -> 0 us
  other arithmetic: 24.2 us -> 0 us
  between operations: 13.9 us -> 0.66 us
  local copies, waits for them, and re-layouts: 3.3 us -> 12.5 us
    psum x3 -> x0, waiting for transfers between devices: 284 us -> none  [the longest x1 168 us: on_device(): up_fac = lax.psum(product(up_acc.T, up_hat), 'dp')]
    psum x2 -> x0, blocking collectives: 141 us -> none  [the longest x1 116 us: on_device(): up_gram = lax.psum(product(up_sum.T, up_sum), 'dp')]
    pallas_call x0 -> x1, Pallas kernels: none -> 59.3 us  [on_device(): pl.pallas_call(kernel, out_shape=(jax.ShapeDtypeStruct((BLK, wide), F32),...]
    dot_general x8 -> x0, matrix products: 26.1 us -> none  [product(): jnp.dot(left, right, precision=highest, preferred_element_type=jnp.float32)]
    another operation x10 -> x0, other arithmetic: 24.1 us -> none  [the longest x6 13 us: factor_basis(): lower = jnp.linalg.cholesky(gram)]
    unnamed x18, local copies, waits for them, and re-layouts: 3.15 us -> 12.5 us
  transfers between devices with their start and end apart: 3 -> 0, of which waited for: 3 -> 0; matrix products, arithmetic and copies ran while one was open for 2% -> 0% of each run, Pallas kernels for 0% -> 0%
where the time goes in v1:
time: 72.7 us; the launch traced here: 72.4 us
  Pallas kernels  59.3 us (82%)
  local copies, waits for them, and re-layouts  12.5 us (17%)
    pallas_call x1, Pallas kernels, on_device(): pl.pallas_call(kernel, out_shape=(jax.ShapeDtypeStruct((BLK, wide), F32),...  59.3 us
    unnamed x18, local copies, waits for them, and re-layouts  12.5 us

profile of v1, /device:TPU:1, one launch (start us, length us, event | category | flops | bytes accessed | tf_op | source)
XLA Modules:
  0.0 72.4 jit_solution(12306321635853502569)
XLA Ops:
  0.6 0.0 copy-start
  0.6 1.5 %copy-done = f32[256,1792]{1,0:T(8,128)S(1)} copy-done((f32[256,1792]{1,0:T(8,128)S(1)}, f32[256,1792]{1,0:T(8,128)}, u32[]{:S(2)}) %copy-start) | copy-done | bytes 1835032
  2.1 0.0 copy-start.1
  2.1 1.5 %copy-done.1 = f32[1792,256]{1,0:T(8,128)S(1)} copy-done((f32[1792,256]{1,0:T(8,128)S(1)}, f32[1792,256]{1,0:T(8,128)}, u32[]{:S(2)}) %copy-start.1) | copy-done | bytes 1835032
  3.6 0.0 copy-start.2
  3.6 1.2 %copy-done.2 = bf16[256,1792]{1,0:T(8,128)(2,1)S(1)} copy-done((bf16[256,1792]{1,0:T(8,128)(2,1)S(1)}, bf16[256,1792]{1,0:T(8,128)(2,1)}, u32[]{:S(2)}) %copy-start.2) | copy-done | bytes 917528
  4.8 0.0 copy-start.3
  4.8 1.2 %copy-done.3 = bf16[1792,256]{1,0:T(8,128)(2,1)S(1)} copy-done((bf16[1792,256]{1,0:T(8,128)(2,1)S(1)}, bf16[1792,256]{1,0:T(8,128)(2,1)}, u32[]{:S(2)}) %copy-start.3) | copy-done | bytes 917528
  6.0 0.0 copy-start.4
  6.0 1.0 %copy-done.4 = f32[1792,64]{0,1:T(8,128)S(1)} copy-done((f32[1792,64]{0,1:T(8,128)S(1)}, f32[1792,64]{0,1:T(8,128)}, u32[]{:S(2)}) %copy-start.4) | copy-done | bytes 458776
  7.0 0.0 copy-start.5
  7.0 0.8 %copy-done.5 = f32[256,64]{0,1:T(8,128)S(1)} copy-done((f32[256,64]{0,1:T(8,128)S(1)}, f32[256,64]{0,1:T(8,128)}, u32[]{:S(2)}) %copy-start.5) | copy-done | bytes 65560
  7.9 59.3 %shard_map.109 = (f32[256,1792]{1,0:T(8,128)S(1)}, f32[1792,256]{1,0:T(8,128)S(1)}, f32[64,256]{1,0:T(8,128)S(1)}, f32[64,1792]{1,0:T(8,128)S(1)}, f32[64,1792]{1,0:T(8,128)S(1)}, /*index=5*/f32[64,256]{1,0:T(8,128)S(1)}) custom-call(bf16[256,1792]{1,0:T(8,128)(2,1)S(1)} %copy-done.2, f32[256,1792]{1,0:T(8,128)S(1)} %copy-done, f32[64,1792]{1,0:T(8,128)S(1)} %bitcast.6, ...), custom_call_target="tpu_custom_call" | custom-call | tf_op jit(solution)/shard_map/pallas_call | solution.py:383
  67.2 1.2 %copy.18 = f32[256,1792]{1,0:T(8,128)} copy(f32[256,1792]{1,0:T(8,128)S(1)} %get-tuple-element.24) | data formatting | bytes 3670016
  68.4 1.2 %copy.19 = f32[1792,256]{1,0:T(8,128)} copy(f32[1792,256]{1,0:T(8,128)S(1)} %get-tuple-element.25) | data formatting | bytes 3670016
  69.6 0.6 copy.20
  70.2 0.8 %copy.21 = f32[1792,64]{0,1:T(8,128)} copy(f32[1792,64]{0,1:T(8,128)S(1)} %bitcast.8) | data formatting | bytes 917504
  71.0 0.8 %copy.22 = f32[1792,64]{0,1:T(8,128)} copy(f32[1792,64]{0,1:T(8,128)S(1)} %bitcast.7) | data formatting | bytes 917504
  71.8 0.6 copy.23
Async XLA Ops:
  0.6 1.5 %copy-start = (f32[256,1792]{1,0:T(8,128)S(1)}, f32[256,1792]{1,0:T(8,128)}, u32[]{:S(2)}) copy-start(f32[256,1792]{1,0:T(8,128)} %eu.1) | copy-start | bytes 5505028
  2.1 1.5 %copy-start.1 = (f32[1792,256]{1,0:T(8,128)S(1)}, f32[1792,256]{1,0:T(8,128)}, u32[]{:S(2)}) copy-start(f32[1792,256]{1,0:T(8,128)} %ed.1) | copy-start | bytes 5505028
  3.6 1.2 %copy-start.2 = (bf16[256,1792]{1,0:T(8,128)(2,1)S(1)}, bf16[256,1792]{1,0:T(8,128)(2,1)}, u32[]{:S(2)}) copy-start(bf16[256,1792]{1,0:T(8,128)(2,1)} %gu.1) | copy-start | bytes 2752516
  4.8 1.2 %copy-start.3 = (bf16[1792,256]{1,0:T(8,128)(2,1)S(1)}, bf16[1792,256]{1,0:T(8,128)(2,1)}, u32[]{:S(2)}) copy-start(bf16[1792,256]{1,0:T(8,128)(2,1)} %gd.1) | copy-start | bytes 2752516
  6.0 1.0 %copy-start.4 = (f32[1792,64]{0,1:T(8,128)S(1)}, f32[1792,64]{0,1:T(8,128)}, u32[]{:S(2)}) copy-start(f32[1792,64]{0,1:T(8,128)} %param.8) | copy-start | bytes 1376260
  7.0 0.8 %copy-start.5 = (f32[256,64]{0,1:T(8,128)S(1)}, f32[256,64]{0,1:T(8,128)}, u32[]{:S(2)}) copy-start(f32[256,64]{0,1:T(8,128)} %param.11) | copy-start | bytes 196612

commit v2 on v1

--- a/solution.py
+++ b/solution.py
@@ -55,19 +55,24 @@
     for i in range(8):
         eye = (lane[:, :RANK] == sub[:, :RANK] + 8 * i).astype(F32)
         groups.append(jnp.concatenate([eye, g[8 * i : 8 * i + 8]], axis=1))
-    scales = [jnp.ones((8, 128), F32) for _ in range(8)]
-    for k in range(RANK):
-        b, r = k // 8, k % 8
-        row = jnp.broadcast_to(groups[b][r : r + 1, :], (8, 128))
-        pivot = jnp.broadcast_to(groups[b][r : r + 1, RANK + k : RANK + k + 1], (8, 128))
-        scales[b] = jnp.where(sub == r, 1.0 / jnp.sqrt(pivot), scales[b])
-        scaled = row * (1.0 / pivot)
-        for i in range(b, 8):
-            col = jnp.broadcast_to(groups[i][:, RANK + k : RANK + k + 1], (8, 128))
-            if i == b:
-                col = jnp.where(sub > r, col, 0.0)
-            groups[i] = groups[i] - col * scaled
-    return jnp.concatenate([groups[i][:, :RANK] * scales[i][:, :RANK] for i in range(8)], axis=0)
+    rows = []
+    for b in range(8):
+        cols = [[jnp.broadcast_to(groups[i][:, RANK + 8*b + j : RANK + 8*b + j + 1], (8, 128)) for i in range(b, 8)] for j in range(8)]
+        pivots = jnp.ones((8, 128), F32)
+        for r in range(8):
+            pivot = jnp.broadcast_to(cols[r][0][r : r + 1, :], (8, 128))
+            inv = 1.0 / pivot
+            pivots = jnp.where(sub == r, pivot, pivots)
+            f = [c * inv for c in cols[r]]
+            f[0] = jnp.where(sub > r, f[0], 0.0)
+            for j in range(r + 1, 8):
+                cj = jnp.broadcast_to(cols[r][0][j : j + 1, :], (8, 128))
+                cols[j] = [cols[j][i] - f[i] * cj for i in range(8 - b)]
+            row = jnp.broadcast_to(groups[b][r : r + 1, :], (8, 128))
+            for i in range(b, 8):
+                groups[i] = groups[i] - f[i - b] * row
+        rows.append(groups[b][:, :RANK] * (1.0 / jnp.sqrt(pivots))[:, :RANK])
+    return jnp.concatenate(rows, axis=0)
 
 
 def triple_left(a):
@@ -90,7 +95,7 @@
     gub, eub, uh, ul, gdb, edb, dh, dl, bub, bdb,
     src, rx, tx, zrx, out,
     part, crx, half, yb, gpart, gx, gz, gsum, gt,
-    sem_load, sem_store, sem_base,
+    sem_load, sem_base,
     s_x, s_z, s_ag, r_x, r_z, r_zag, r_xag,
     s_c, r_c, s_y, r_y, s_g, r_g,
 ):
@@ -344,24 +349,17 @@
     right_d = dot(inv_d, triple_right(y_sum(1)), NN)
     wd[...] = right_d
     right_d3 = triple_right(right_d)
-    stores = []
     for j in range(NB):
         left = dot(inv_d, triple_right(out[0, j]), NN)
         ld[:, j * BLK : (j + 1) * BLK] = left
-        edb[j] = edb[j] - dot(triple_left(left.T), right_d3, NN)
-        store = pltpu.make_async_copy(edb.at[j], rd.at[pl.ds(j * BLK, BLK), :], sem_store.at[0, j])
-        store.start()
-        stores.append(store)
+        rd[j * BLK : (j + 1) * BLK, :] = edb[j] - dot(triple_left(left.T), right_d3, NN)
 
     for i in reversed(range(NB)):
         gathered(1, i)
     for j in range(NB):
         right = dot(inv_u, triple_right(out[1, j]), NN)
         wu[:, j * BLK : (j + 1) * BLK] = right
-        eub[j] = eub[j] - dot(left_u_t, triple_right(right), NN)
-        store = pltpu.make_async_copy(eub.at[j], ru.at[:, pl.ds(j * BLK, BLK)], sem_store.at[1, j])
-        store.start()
-        stores.append(store)
+        ru[:, j * BLK : (j + 1) * BLK] = eub[j] - dot(left_u_t, triple_right(right), NN)
 
     dp_sends_done(0)
     dp_sends_done(1)
@@ -371,12 +369,32 @@
     wait_bytes(gz.at[pl.ds(0, 3)], s_g.at[0])
     wait_bytes(gz.at[pl.ds(0, 7)], s_g.at[1])
     wait_bytes(gz.at[pl.ds(0, 7)], s_g.at[2])
-    for store in stores:
-        store.wait()
+
+
+def store_kernel(*refs):
+    n = len(refs) // 2
+    sems = refs[2 * n]
+    copies = [pltpu.make_async_copy(refs[i], refs[n + i], sems.at[i]) for i in range(n)]
+    for copy in copies:
+        copy.start()
+    for copy in copies:
+        copy.wait()
+
+
+def store_all(*arrays):
+    return pl.pallas_call(
+        store_kernel,
+        out_shape=tuple(jax.ShapeDtypeStruct(a.shape, a.dtype) for a in arrays),
+        in_specs=[pl.BlockSpec(memory_space=pl.ANY)] * len(arrays),
+        out_specs=(pl.BlockSpec(memory_space=pltpu.HBM),) * len(arrays),
+        scratch_shapes=[pltpu.SemaphoreType.DMA((len(arrays),))],
+        compiler_params=pltpu.CompilerParams(vmem_limit_bytes=2**20),
+    )(*arrays)
 
 
 def on_device(up_grad, up_error, up_basis, down_grad, down_error, down_basis):
-    any_space = pl.BlockSpec(memory_space=pl.ANY)
+    arrays = (up_grad, up_error, up_basis.T, down_grad, down_error, down_basis.T)
+    hbm = pl.BlockSpec(memory_space=pltpu.HBM)
     vmem = pl.BlockSpec(memory_space=pltpu.VMEM)
     dma = pltpu.SemaphoreType.DMA
     wide = NB * BLK
@@ -390,8 +408,8 @@
             jax.ShapeDtypeStruct((RANK, wide), F32),
             jax.ShapeDtypeStruct((RANK, BLK), F32),
         ),
-        in_specs=[any_space] * 6,
-        out_specs=(any_space, any_space, vmem, vmem, vmem, vmem),
+        in_specs=[hbm] * 6,
+        out_specs=(vmem,) * 6,
         scratch_shapes=[
             pltpu.VMEM((NB, BLK, BLK), BF16),
             pltpu.VMEM((NB, BLK, BLK), F32),
@@ -418,7 +436,6 @@
             pltpu.VMEM((RANK // 2, 128), F32),
             pltpu.VMEM((NY * NC, RANK // 2, 128), F32),
             dma((4, NB)),
-            dma((2, NB)),
             dma((2,)),
             dma((2,)),
             dma((2,)),
@@ -437,7 +454,8 @@
         compiler_params=pltpu.CompilerParams(
             collective_id=0, has_side_effects=True, vmem_limit_bytes=32 * 2**20
         ),
-    )(up_grad, up_error, up_basis.T, down_grad, down_error, down_basis.T)
+    )(*(pltpu.with_memory_space_constraint(a, pltpu.HBM) for a in arrays))
+    ru, rd, lu, wu, ld, wd = store_all(ru, rd, lu, wu, ld, wd)
     return ru, rd, lu.T, wu.T, ld.T, wd.T
 
 

time: 72.7 us -> 47.4 us (0.65)
  Pallas kernels: 59.3 us -> 46.7 us
  local copies, waits for them, and re-layouts: 12.5 us -> 0 us
    pallas_call x1, Pallas kernels: 59.3 us -> 44.5 us  [on_device(): pl.pallas_call(kernel, out_shape=(jax.ShapeDtypeStruct((BLK, wide), F32),...]
    unnamed x18 -> x0, local copies, waits for them, and re-layouts: 12.5 us -> none
    pallas_call x0 -> x1, Pallas kernels: none -> 2.2 us  [store_all(): pl.pallas_call(store_kernel, out_shape=tuple((jax.ShapeDtypeStruct(a.shap...]
where the time goes in v2:
time: 47.4 us; the launch traced here: 47.3 us
  Pallas kernels  46.7 us (99%)
  between operations  0.64 us (1%)
    pallas_call x1, Pallas kernels, on_device(): pl.pallas_call(kernel, out_shape=(jax.ShapeDtypeStruct((BLK, wide), F32),...  44.5 us
    pallas_call x1, Pallas kernels, store_all(): pl.pallas_call(store_kernel, out_shape=tuple((jax.ShapeDtypeStruct(a.shap...  2.2 us

profile of v2, /device:TPU:1, one launch (start us, length us, event | category | flops | bytes accessed | tf_op | source)
XLA Modules:
  0.0 47.3 jit_solution(10892577975445470143)
XLA Ops:
  0.6 44.5 %shard_map.109 = (f32[256,1792]{1,0:T(8,128)S(1)}, f32[1792,256]{1,0:T(8,128)S(1)}, f32[64,256]{1,0:T(8,128)S(1)}, f32[64,1792]{1,0:T(8,128)S(1)}, f32[64,1792]{1,0:T(8,128)S(1)}, /*index=5*/f32[64,256]{1,0:T(8,128)S(1)}) custom-call(bf16[256,1792]{1,0:T(8,128)(2,1)} %gu.1, f32[256,1792]{1,0:T(8,128)} %eu.1, f32[64,1792]{1,0:T(8,128)} %bitcast.6, ...), custom_call_target="tpu_custom_call" | custom-call | tf_op jit(solution)/shard_map/pallas_call | solution.py:401
  45.1 2.2 %shard_map.110 = (f32[256,1792]{1,0:T(8,128)}, f32[1792,256]{1,0:T(8,128)}, f32[64,256]{1,0:T(8,128)}, f32[64,1792]{1,0:T(8,128)}, f32[64,1792]{1,0:T(8,128)}, /*index=5*/f32[64,256]{1,0:T(8,128)}) custom-call(f32[256,1792]{1,0:T(8,128)S(1)} %get-tuple-element.18.refs_0_, f32[1792,256]{1,0:T(8,128)S(1)} %get-tuple-element.19.refs_1_, ...), custom_call_target="tpu_custom_call" | custom-call | tf_op jit(solution)/shard_map/pallas_call | solution.py:385

commit v3 on v2

--- a/solution.py
+++ b/solution.py
@@ -91,10 +91,10 @@
 
 def kernel(
     gu, eu, bu, gd, ed, bd,
-    ru, rd, lu, wu, ld, wd,
-    gub, eub, uh, ul, gdb, edb, dh, dl, bub, bdb,
+    rd, lu, ld, wd, eub, w_out, inv_out, left_out,
+    gub, uh, ul, gdb, edb, dh, dl, bub, bdb,
     src, rx, tx, zrx, out,
-    part, crx, half, yb, gpart, gx, gz, gsum, gt,
+    part, crx, half, yb, gpart, gx, gz, gsum, gt, lt,
     sem_load, sem_base,
     s_x, s_z, s_ag, r_x, r_z, r_zag, r_xag,
     s_c, r_c, s_y, r_y, s_g, r_g,
@@ -244,162 +244,198 @@
             halves.append(total)
         return jnp.concatenate(halves, axis=0)
 
-    base_d.wait()
-    bd_hi, bd_lo = split(bdb[...])
-    bd_cat = jnp.concatenate([bd_hi, bd_lo], axis=0)
-    for i in range(NB):
-        j = order[i]
-        loads_d[i][0].wait()
-        loads_d[i][1].wait()
-        acc = gdb[j].astype(F32) + edb[j]
-        edb[j] = acc
-        hi, lo = split(acc)
-        dh[j] = hi
-        dl[j] = lo
-        src[0, j] = product3(bd_cat, bd_hi, hi, lo, NT)
-    pl.semaphore_wait(barrier, len(peers))
-    for i in range(NB):
-        x_send(0, i)
-
-    base_u.wait()
-    total = jnp.zeros((RANK, BLK), F32)
-    for j in range(NB):
-        loads_u[j][0].wait()
-        loads_u[j][1].wait()
-        acc = gub[j].astype(F32) + eub[j]
-        eub[j] = acc
-        hi, lo = split(acc)
-        uh[j] = hi
-        ul[j] = lo
-        b_hi, b_lo = split(bub[:, j * BLK : (j + 1) * BLK])
-        total = total + product3(jnp.concatenate([b_hi, b_lo], axis=0), b_hi, hi, lo, NT)
-    part[0, 0] = total[:32]
-    part[0, 1] = total[32:]
+    keep = {}
+
+    def part_down():
+        base_d.wait()
+        hi_b, lo_b = split(bdb[...])
+        cat = jnp.concatenate([hi_b, lo_b], axis=0)
+        for i in range(NB):
+            j = order[i]
+            loads_d[i][0].wait()
+            loads_d[i][1].wait()
+            acc = gdb[j].astype(F32) + edb[j]
+            edb[j] = acc
+            hi, lo = split(acc)
+            dh[j] = hi
+            dl[j] = lo
+            src[0, j] = product3(cat, hi_b, hi, lo, NT)
+            x_send(0, i)
+
+    def part_up():
+        base_u.wait()
+        total = jnp.zeros((RANK, BLK), F32)
+        for j in range(NB):
+            loads_u[j][0].wait()
+            loads_u[j][1].wait()
+            acc = gub[j].astype(F32) + eub[j]
+            eub[j] = acc
+            hi, lo = split(acc)
+            uh[j] = hi
+            ul[j] = lo
+            hi_b, lo_b = split(bub[:, j * BLK : (j + 1) * BLK])
+            total = total + product3(jnp.concatenate([hi_b, lo_b], axis=0), hi_b, hi, lo, NT)
+        part[0, 0] = total[:32]
+        part[0, 1] = total[32:]
+
+    def enter():
+        pl.semaphore_wait(barrier, len(peers))
+
+    def z_sends(a):
+        for i in range(NB):
+            z_send(a, i)
+
+    def gram_up_x():
+        xu = y_sum(0)
+        keep["xu"] = xu
+        hi, lo = split(xu)
+        cat = jnp.concatenate([hi, lo], axis=0)
+        keep["xu_split"] = (hi, cat)
+        g = pack(gram(cat))
+        gpart[0] = g
+        gx[x] = g
+        for d in (2, 1, 3):
+            copy_to(gpart.at[0], gx.at[x], s_g.at[0], r_g.at[0], to_x(d))
+
+    def second_up():
+        hi, cat = keep["xu_split"]
+        for i in range(NB):
+            j = order[i]
+            src[1, j] = product3(cat, hi, uh[j], ul[j], NN)
+            x_send(1, i)
+
+    def gram_up_z():
+        wait_bytes(gx.at[pl.ds(0, 3)], r_g.at[0])
+        g = gx[0] + gx[1] + gx[2] + gx[3]
+        gsum[...] = g
+        gz[z] = g
+        for d in (4, 3, 5, 2, 6, 1, 7):
+            copy_to(gsum, gz.at[z], s_g.at[1], r_g.at[1], to_z(lax.rem(z + d, NZ)))
+
+    def second_down():
+        prod = jnp.zeros((RANK, BLK), F32)
+        gsq = jnp.zeros((RANK, RANK), F32)
+        for i in reversed(range(NB)):
+            gathered(0, i)
+        for j in range(NB):
+            hi, lo = split(out[0, j])
+            cat = jnp.concatenate([hi, lo], axis=0)
+            gsq = gsq + gram(cat)
+            prod = prod + product3(cat, hi, dh[j], dl[j], NN)
+        g = pack(gsq)
+        gpart[1] = g
+        gt[t] = g
+        part[1, 0] = prod[:32]
+        part[1, 1] = prod[32:]
+        c_send(1)
+        for dy, dc in others_t:
+            copy_to(gpart.at[1], gt.at[t], s_g.at[2], r_g.at[2], to_t(dy, dc))
+
+    def factor_up():
+        wait_bytes(gz.at[pl.ds(0, 7)], r_g.at[1])
+        g = gz[0]
+        for s in range(1, NZ):
+            g = g + gz[s]
+        keep["inv_u"] = triple_left(inverse_factor(unpack(g)))
+        left = dot(keep["inv_u"], triple_right(keep["xu"]), NN)
+        lu[...] = left
+        keep["left_u"] = triple_left(left.T)
+
+    def factor_down():
+        wait_bytes(gt.at[pl.ds(0, 7)], r_g.at[2])
+        g = gt[0]
+        for s in range(1, NY * NC):
+            g = g + gt[s]
+        keep["inv_d"] = triple_left(inverse_factor(unpack(g)))
+
+    def left_down():
+        for j in range(NB):
+            left = dot(keep["inv_d"], triple_right(out[0, j]), NN)
+            ld[:, j * BLK : (j + 1) * BLK] = left
+            lt[j] = triple_left(left.T)
+
+    def last_down():
+        right = dot(keep["inv_d"], triple_right(y_sum(1)), NN)
+        wd[...] = right
+        right = triple_right(right)
+        for j in range(NB):
+            rd[j * BLK : (j + 1) * BLK, :] = edb[j] - dot(lt[j], right, NN)
+
+    def tensor_sends_done(a):
+        wait_bytes(crx.at[a], s_c.at[a])
+        wait_bytes(yb.at[a, pl.ds(0, 7)], s_y.at[a])
+
+    enter()
+    part_down()
+    part_up()
     c_send(0)
     y_send(0)
-
-    for i in range(NB):
-        z_send(0, i)
-
-    xu = y_sum(0)
-    xu_hi, xu_lo = split(xu)
-    xu_cat = jnp.concatenate([xu_hi, xu_lo], axis=0)
-    g = pack(gram(xu_cat))
-    gpart[0] = g
-    gx[x] = g
-    for d in (2, 1, 3):
-        copy_to(gpart.at[0], gx.at[x], s_g.at[0], r_g.at[0], to_x(d))
-    for i in range(NB):
-        j = order[i]
-        src[1, j] = product3(xu_cat, xu_hi, uh[j], ul[j], NN)
-        x_send(1, i)
-
+    z_sends(0)
+    gram_up_x()
+    second_up()
     reduce_gather(0)
-
-    wait_bytes(gx.at[pl.ds(0, 3)], r_g.at[0])
-    g = gx[0] + gx[1] + gx[2] + gx[3]
-    gsum[...] = g
-    gz[z] = g
-    for d in (4, 3, 5, 2, 6, 1, 7):
-        copy_to(gsum, gz.at[z], s_g.at[1], r_g.at[1], to_z(lax.rem(z + d, NZ)))
-
-    for i in reversed(range(NB)):
+    gram_up_z()
+    for i in (6, 5, 4):
         forward(0, i)
-    for i in range(NB):
+    for i in range(4):
         z_send(1, i)
-
-    prod = jnp.zeros((RANK, BLK), F32)
-    gsq = jnp.zeros((RANK, RANK), F32)
-    for i in reversed(range(NB)):
-        gathered(0, i)
-    for j in range(NB):
-        hi, lo = split(out[0, j])
-        cat = jnp.concatenate([hi, lo], axis=0)
-        gsq = gsq + gram(cat)
-        prod = prod + product3(cat, hi, dh[j], dl[j], NN)
-    g = pack(gsq)
-    gpart[1] = g
-    gt[t] = g
-    for dy, dc in others_t:
-        copy_to(gpart.at[1], gt.at[t], s_g.at[2], r_g.at[2], to_t(dy, dc))
-    part[1, 0] = prod[:32]
-    part[1, 1] = prod[32:]
-    c_send(1)
-
+        forward(0, 3 - i)
+    for i in (4, 5, 6):
+        z_send(1, i)
+    factor_up()
     reduce_gather(1)
+    second_down()
+    for i in (6, 5):
+        forward(1, i)
     y_send(1)
-
-    wait_bytes(gz.at[pl.ds(0, 7)], r_g.at[1])
-    g = gz[0]
-    for s in range(1, NZ):
-        g = g + gz[s]
-    inv_u = triple_left(inverse_factor(unpack(g)))
-    left_u = dot(inv_u, triple_right(xu), NN)
-    lu[...] = left_u
-    left_u_t = triple_left(left_u.T)
-
-    for i in reversed(range(NB)):
+    for i in (4, 3, 2, 1, 0):
         forward(1, i)
-
-    wait_bytes(gt.at[pl.ds(0, 7)], r_g.at[2])
-    g = gt[0]
-    for s in range(1, NY * NC):
-        g = g + gt[s]
-    inv_d = triple_left(inverse_factor(unpack(g)))
-    right_d = dot(inv_d, triple_right(y_sum(1)), NN)
-    wd[...] = right_d
-    right_d3 = triple_right(right_d)
-    for j in range(NB):
-        left = dot(inv_d, triple_right(out[0, j]), NN)
-        ld[:, j * BLK : (j + 1) * BLK] = left
-        rd[j * BLK : (j + 1) * BLK, :] = edb[j] - dot(triple_left(left.T), right_d3, NN)
-
+    factor_down()
+    left_down()
+    last_down()
+    dp_sends_done(0)
+    tensor_sends_done(0)
+    wait_bytes(gz.at[pl.ds(0, 3)], s_g.at[0])
+    wait_bytes(gz.at[pl.ds(0, 7)], s_g.at[1])
+    tensor_sends_done(1)
+    wait_bytes(gz.at[pl.ds(0, 7)], s_g.at[2])
+    inv_out[...] = keep["inv_u"]
+    left_out[...] = keep["left_u"]
     for i in reversed(range(NB)):
         gathered(1, i)
-    for j in range(NB):
-        right = dot(inv_u, triple_right(out[1, j]), NN)
-        wu[:, j * BLK : (j + 1) * BLK] = right
-        ru[:, j * BLK : (j + 1) * BLK] = eub[j] - dot(left_u_t, triple_right(right), NN)
-
-    dp_sends_done(0)
+    w_out[...] = out[1]
     dp_sends_done(1)
-    for a in range(2):
-        wait_bytes(crx.at[a], s_c.at[a])
-        wait_bytes(yb.at[a, pl.ds(0, 7)], s_y.at[a])
-    wait_bytes(gz.at[pl.ds(0, 3)], s_g.at[0])
-    wait_bytes(gz.at[pl.ds(0, 7)], s_g.at[1])
-    wait_bytes(gz.at[pl.ds(0, 7)], s_g.at[2])
-
-
-def store_kernel(*refs):
-    n = len(refs) // 2
-    sems = refs[2 * n]
-    copies = [pltpu.make_async_copy(refs[i], refs[n + i], sems.at[i]) for i in range(n)]
+
+
+def store_kernel(rd, lu, ld, wd, acc, w, inv, left, o_ru, o_rd, o_lu, o_wu, o_ld, o_wd, ru, wu, sems, sems_u):
+    copies = [
+        pltpu.make_async_copy(a, b, sems.at[i])
+        for i, (a, b) in enumerate(((rd, o_rd), (ld, o_ld), (lu, o_lu), (wd, o_wd)))
+    ]
     for copy in copies:
         copy.start()
+    rights = [dot(inv[...], triple_right(w[j]), NN) for j in range(NB)]
+    for j in range(NB):
+        cut = pl.ds(j * BLK, BLK)
+        right = rights[j]
+        wu[:, cut] = right
+        ru[:, cut] = acc[j] - dot(left[...], triple_right(right), NN)
+        copy = pltpu.make_async_copy(ru.at[:, cut], o_ru.at[:, cut], sems_u.at[j])
+        copy.start()
+        copies.append(copy)
+    copy = pltpu.make_async_copy(wu, o_wu, sems.at[4])
+    copy.start()
+    copies.append(copy)
     for copy in copies:
         copy.wait()
 
 
 def store_all(*arrays):
+    wide = NB * BLK
+    vmem = pl.BlockSpec(memory_space=pltpu.VMEM)
+    dma = pltpu.SemaphoreType.DMA
     return pl.pallas_call(
         store_kernel,
-        out_shape=tuple(jax.ShapeDtypeStruct(a.shape, a.dtype) for a in arrays),
-        in_specs=[pl.BlockSpec(memory_space=pl.ANY)] * len(arrays),
-        out_specs=(pl.BlockSpec(memory_space=pltpu.HBM),) * len(arrays),
-        scratch_shapes=[pltpu.SemaphoreType.DMA((len(arrays),))],
-        compiler_params=pltpu.CompilerParams(vmem_limit_bytes=2**20),
-    )(*arrays)
-
-
-def on_device(up_grad, up_error, up_basis, down_grad, down_error, down_basis):
-    arrays = (up_grad, up_error, up_basis.T, down_grad, down_error, down_basis.T)
-    hbm = pl.BlockSpec(memory_space=pltpu.HBM)
-    vmem = pl.BlockSpec(memory_space=pltpu.VMEM)
-    dma = pltpu.SemaphoreType.DMA
-    wide = NB * BLK
-    ru, rd, lu, wu, ld, wd = pl.pallas_call(
-        kernel,
         out_shape=(
             jax.ShapeDtypeStruct((BLK, wide), F32),
             jax.ShapeDtypeStruct((wide, BLK), F32),
@@ -408,11 +444,40 @@
             jax.ShapeDtypeStruct((RANK, wide), F32),
             jax.ShapeDtypeStruct((RANK, BLK), F32),
         ),
+        in_specs=[pl.BlockSpec(memory_space=pl.ANY)] * 4 + [vmem] * 4,
+        out_specs=(pl.BlockSpec(memory_space=pltpu.HBM),) * 6,
+        scratch_shapes=[
+            pltpu.VMEM((BLK, wide), F32),
+            pltpu.VMEM((RANK, wide), F32),
+            dma((5,)),
+            dma((NB,)),
+        ],
+        compiler_params=pltpu.CompilerParams(vmem_limit_bytes=16 * 2**20),
+    )(*arrays)
+
+
+def on_device(up_grad, up_error, up_basis, down_grad, down_error, down_basis):
+    arrays = (up_grad, up_error, up_basis.T, down_grad, down_error, down_basis.T)
+    hbm = pl.BlockSpec(memory_space=pltpu.HBM)
+    vmem = pl.BlockSpec(memory_space=pltpu.VMEM)
+    dma = pltpu.SemaphoreType.DMA
+    wide = NB * BLK
+    results = pl.pallas_call(
+        kernel,
+        out_shape=(
+            pltpu.VMEM((wide, BLK), F32),
+            pltpu.VMEM((RANK, BLK), F32),
+            pltpu.VMEM((RANK, wide), F32),
+            pltpu.VMEM((RANK, BLK), F32),
+            pltpu.VMEM((NB, BLK, BLK), F32),
+            pltpu.VMEM((NB, RANK, BLK), F32),
+            pltpu.VMEM((RANK, 3 * RANK), BF16),
+            pltpu.VMEM((BLK, 3 * RANK), BF16),
+        ),
         in_specs=[hbm] * 6,
-        out_specs=(vmem,) * 6,
+        out_specs=(vmem,) * 8,
         scratch_shapes=[
             pltpu.VMEM((NB, BLK, BLK), BF16),
-            pltpu.VMEM((NB, BLK, BLK), F32),
             pltpu.VMEM((NB, BLK, BLK), BF16),
             pltpu.VMEM((NB, BLK, BLK), BF16),
             pltpu.VMEM((NB, BLK, BLK), BF16),
@@ -435,6 +500,7 @@
             pltpu.VMEM((NZ, RANK // 2, 128), F32),
             pltpu.VMEM((RANK // 2, 128), F32),
             pltpu.VMEM((NY * NC, RANK // 2, 128), F32),
+            pltpu.VMEM((NB, BLK, 3 * RANK), BF16),
             dma((4, NB)),
             dma((2,)),
             dma((2,)),
@@ -455,7 +521,7 @@
             collective_id=0, has_side_effects=True, vmem_limit_bytes=32 * 2**20
         ),
     )(*(pltpu.with_memory_space_constraint(a, pltpu.HBM) for a in arrays))
-    ru, rd, lu, wu, ld, wd = store_all(ru, rd, lu, wu, ld, wd)
+    ru, rd, lu, wu, ld, wd = store_all(*results)
     return ru, rd, lu.T, wu.T, ld.T, wd.T
 
 

time: 47.4 us -> 45 us (0.949)
  Pallas kernels: 46.7 us -> 44.3 us
    pallas_call x2, Pallas kernels: 46.7 us -> 44.3 us  [the longest x1 42 us: on_device(): pl.pallas_call(kernel, out_shape=(pltpu.VMEM((wide, BLK), F32), pltpu.VME...]
where the time goes in v3:
time: 45 us; the launch traced here: 44.9 us
  Pallas kernels  44.3 us (98%)
  between operations  0.64 us (1%)
    pallas_call x1, Pallas kernels, on_device(): pl.pallas_call(kernel, out_shape=(pltpu.VMEM((wide, BLK), F32), pltpu.VME...  42 us
    pallas_call x1, Pallas kernels, store_all(): pl.pallas_call(store_kernel, out_shape=(jax.ShapeDtypeStruct((BLK, wide),...  2.27 us

profile of v3, /device:TPU:1, one launch (start us, length us, event | category | flops | bytes accessed | tf_op | source)
XLA Modules:
  0.0 44.9 jit_solution(11003847478368516861)
XLA Ops:
  0.6 42.0 %shard_map.109 = (f32[1792,256]{1,0:T(8,128)S(1)}, f32[64,256]{1,0:T(8,128)S(1)}, f32[64,1792]{1,0:T(8,128)S(1)}, f32[64,256]{1,0:T(8,128)S(1)}, f32[7,256,256]{...) custom-call(bf16[256,1792]{1,0:T(8,128)(2,1)} %gu.1, ...), custom_call_target="tpu_custom_call" | custom-call | tf_op jit(solution)/shard_map/pallas_call | solution.py:465
  42.7 2.3 %shard_map.110 = (f32[256,1792]{1,0:T(8,128)}, f32[1792,256]{1,0:T(8,128)}, f32[64,256]{1,0:T(8,128)}, f32[64,1792]{1,0:T(8,128)}, f32[64,1792]{1,0:T(8,128)}, /*index=5*/f32[64,256]{1,0:T(8,128)}) custom-call(f32[1792,256]{1,0:T(8,128)S(1)} %get-tuple-element.20.rd, f32[64,256]{1,0:T(8,128)S(1)} %get-tuple-element.21.lu, ...), custom_call_target="tpu_custom_call" | custom-call | tf_op jit(solution)/shard_map/pallas_call | solution.py:437

commit v4 on v3

--- a/solution.py
+++ b/solution.py
@@ -246,11 +246,14 @@
 
     keep = {}
 
-    def part_down():
+    def base_down():
         base_d.wait()
         hi_b, lo_b = split(bdb[...])
-        cat = jnp.concatenate([hi_b, lo_b], axis=0)
-        for i in range(NB):
+        keep["bd"] = (hi_b, jnp.concatenate([hi_b, lo_b], axis=0))
+
+    def part_down(steps):
+        hi_b, cat = keep["bd"]
+        for i in steps:
             j = order[i]
             loads_d[i][0].wait()
             loads_d[i][1].wait()
@@ -366,10 +369,13 @@
         wait_bytes(yb.at[a, pl.ds(0, 7)], s_y.at[a])
 
     enter()
-    part_down()
+    base_down()
+    part_down((0, 1))
     part_up()
     c_send(0)
+    part_down((2, 3, 4))
     y_send(0)
+    part_down((5, 6))
     z_sends(0)
     gram_up_x()
     second_up()

time: 45 us -> 44.4 us (0.987)
  Pallas kernels: 44.3 us -> 43.7 us
    pallas_call x1, Pallas kernels: 42 us -> 41.4 us  [on_device(): pl.pallas_call(kernel, out_shape=(pltpu.VMEM((wide, BLK), F32), pltpu.VME...]
where the time goes in v4:
time: 44.4 us; the launch traced here: 44.3 us
  Pallas kernels  43.7 us (98%)
  between operations  0.64 us (1%)
    pallas_call x1, Pallas kernels, on_device(): pl.pallas_call(kernel, out_shape=(pltpu.VMEM((wide, BLK), F32), pltpu.VME...  41.4 us
    pallas_call x1, Pallas kernels, store_all(): pl.pallas_call(store_kernel, out_shape=(jax.ShapeDtypeStruct((BLK, wide),...  2.27 us

profile of v4, /device:TPU:1, one launch (start us, length us, event | category | flops | bytes accessed | tf_op | source)
XLA Modules:
  0.0 44.3 jit_solution(11082586360552949884)
XLA Ops:
  0.6 41.4 %shard_map.109 = (f32[1792,256]{1,0:T(8,128)S(1)}, f32[64,256]{1,0:T(8,128)S(1)}, f32[64,1792]{1,0:T(8,128)S(1)}, f32[64,256]{1,0:T(8,128)S(1)}, f32[7,256,256]{...) custom-call(bf16[256,1792]{1,0:T(8,128)(2,1)} %gu.1, ...), custom_call_target="tpu_custom_call" | custom-call | tf_op jit(solution)/shard_map/pallas_call | solution.py:471
  42.0 2.3 %shard_map.110 = (f32[256,1792]{1,0:T(8,128)}, f32[1792,256]{1,0:T(8,128)}, f32[64,256]{1,0:T(8,128)}, f32[64,1792]{1,0:T(8,128)}, f32[64,1792]{1,0:T(8,128)}, /*index=5*/f32[64,256]{1,0:T(8,128)}) custom-call(f32[1792,256]{1,0:T(8,128)S(1)} %get-tuple-element.20.rd, f32[64,256]{1,0:T(8,128)S(1)} %get-tuple-element.21.lu, ...), custom_call_target="tpu_custom_call" | custom-call | tf_op jit(solution)/shard_map/pallas_call | solution.py:443

commit v5 on v4

--- a/solution.py
+++ b/solution.py
@@ -138,14 +138,18 @@
 
     base_d = pltpu.make_async_copy(bd, bdb, sem_base.at[0])
     base_d.start()
-    loads_d = []
-    for i in range(NB):
+    loads_d = {}
+
+    def load_down(i):
         cut = pl.ds(pl.multiple_of(order[i] * BLK, BLK), BLK)
         a = pltpu.make_async_copy(gd.at[cut, :], gdb.at[order[i]], sem_load.at[0, i])
         b = pltpu.make_async_copy(ed.at[cut, :], edb.at[order[i]], sem_load.at[1, i])
         a.start()
         b.start()
-        loads_d.append((a, b))
+        loads_d[i] = (a, b)
+
+    for i in range(2):
+        load_down(i)
     base_u = pltpu.make_async_copy(bu, bub, sem_base.at[1])
     base_u.start()
     loads_u = []
@@ -156,6 +160,8 @@
         a.start()
         b.start()
         loads_u.append((a, b))
+    for i in range(2, NB):
+        load_down(i)
 
     def x_send(a, i):
         j = order[i]

time: 44.4 us -> 44.5 us (level)
  no operation moved by 1% of the time
where the time goes in v5:
time: 44.5 us; the launch traced here: 44.4 us
  Pallas kernels  43.7 us (98%)
  between operations  0.64 us (1%)
    pallas_call x1, Pallas kernels, on_device(): pl.pallas_call(kernel, out_shape=(pltpu.VMEM((wide, BLK), F32), pltpu.VME...  41.5 us
    pallas_call x1, Pallas kernels, store_all(): pl.pallas_call(store_kernel, out_shape=(jax.ShapeDtypeStruct((BLK, wide),...  2.27 us

profile of v5, /device:TPU:1, one launch (start us, length us, event | category | flops | bytes accessed | tf_op | source)
XLA Modules:
  0.0 44.4 jit_solution(4452697554152381048)
XLA Ops:
  0.6 41.5 %shard_map.109 = (f32[1792,256]{1,0:T(8,128)S(1)}, f32[64,256]{1,0:T(8,128)S(1)}, f32[64,1792]{1,0:T(8,128)S(1)}, f32[64,256]{1,0:T(8,128)S(1)}, f32[7,256,256]{...) custom-call(bf16[256,1792]{1,0:T(8,128)(2,1)} %gu.1, ...), custom_call_target="tpu_custom_call" | custom-call | tf_op jit(solution)/shard_map/pallas_call | solution.py:477
  42.1 2.3 %shard_map.110 = (f32[256,1792]{1,0:T(8,128)}, f32[1792,256]{1,0:T(8,128)}, f32[64,256]{1,0:T(8,128)}, f32[64,1792]{1,0:T(8,128)}, f32[64,1792]{1,0:T(8,128)}, /*index=5*/f32[64,256]{1,0:T(8,128)}) custom-call(f32[1792,256]{1,0:T(8,128)S(1)} %get-tuple-element.20.rd, f32[64,256]{1,0:T(8,128)S(1)} %get-tuple-element.21.lu, ...), custom_call_target="tpu_custom_call" | custom-call | tf_op jit(solution)/shard_map/pallas_call | solution.py:449
